TPU v7x, 768 devices: a whole 4x8x12 slice. The times are simulated.
768 devices in a mesh: row: 64 (over y, x, core), col: 12 (over z).
Axes of the slice: x: 4, y: 8, z: 12, core: 2. Of those that a mesh axis runs over, the one named last changes fastest.
Arguments:
- a_tiles: bfloat16 [256, 24, 128, 128], P('row', 'col'), may hold values from -28 to 28
- block_owner: int32 [256, 24], P('row', 'col'), may hold values from 0 to 63, as said below
- send_rows: int32 [64, 64], replicated, may hold values from 0 to 3
- stripe: bfloat16 [32768, 3072], P('row', 'col'), may hold values from -0.109375 to 0.109375
Outputs:
- inflated: float32 [32768, 3072], P('row', 'col')
Inputs may be any that keep to these rules, and one draw needn't show every extreme that they name: `block_owner`: each value names an index along row.
All inputs are finite; a program needn't handle non-finite values.
Results may differ from a plain program's by a relative error of at most 0.0003.
Values may be sent and summed in bfloat16 or wider, within the bound.
A program may use at most 64 MiB of HBM per device.

v0:
```python
import jax
import jax.numpy as jnp
from jax import lax
from jax.sharding import PartitionSpec as P


def local(a_tiles, block_owner, send_rows, stripe):
    tile_edge = a_tiles.shape[-1]
    stripe_width = stripe.shape[1]
    local_rows = a_tiles.shape[0]
    owners = lax.axis_size("row")
    my_index = lax.axis_index("row")
    my_column = lax.dynamic_slice_in_dim(send_rows, my_index, 1, 1)[:, 0]
    shard_rows = local_rows * tile_edge
    portion = lax.all_gather(stripe, "row", axis=0, tiled=True)
    count = portion.shape[0] // shard_rows

    def place(step, held):
        start = step * shard_rows + my_column[step] * tile_edge
        picked = lax.dynamic_slice_in_dim(portion, start, tile_edge, 0)
        zero = jnp.zeros((), jnp.int32)
        return lax.dynamic_update_slice(held, picked[None], (step, zero, zero))

    fetched = lax.fori_loop(
        0, count, place, jnp.zeros((owners, tile_edge, stripe_width), jnp.bfloat16)
    )
    left_tiles = lax.all_gather(a_tiles, "col", axis=1, tiled=True)
    owner_index = lax.all_gather(block_owner, "col", axis=1, tiled=True)
    right_tiles = fetched[owner_index]
    product = jnp.zeros((local_rows, tile_edge, stripe_width), jnp.float32) + jnp.einsum(
        "isab,isbw->iaw", left_tiles, right_tiles, preferred_element_type=jnp.float32
    )
    squared = product * product
    column_sum = lax.psum(jnp.sum(squared, axis=(0, 1)), "row")
    row_count = owners * local_rows * tile_edge
    return (row_count * squared / column_sum).reshape(local_rows * tile_edge, stripe_width)


def solution(mesh):
    placed = (P("row", "col", None, None), P("row", "col"), P(), P("row", "col"))
    return jax.shard_map(
        local, mesh=mesh, in_specs=placed, out_specs=P("row", "col"), check_vma=False
    )
```

profile of v0, /device:TPU:1, one launch (start us, length us, event | category | flops | bytes accessed | tf_op | source)
XLA Modules:
  0.0 455.9 jit_solution(1252449099486568404)
XLA Ops:
  8.0 27.9 %all-gather = s32[12,2,4]{2,1,0:T(2,128)S(1)} all-gather(s32[1,2,4]{2,1,0:T(2,128)} %bitcast.26), channel_id=1, replica_groups=mesh['row'=64,'col'=12] {'col'}, dimensions={0}, use_global_device_ids=true | all-gather | bytes 416 | tf_op jit(solution)/shard_map/all_gather | solution.py:28
  36.3 93.4 %all-gather.4.cloned.1.call-done = bf16[32768,256]{1,0:T(8,128)(2,1)} async-done(((bf16[512,256]{1,0:T(8,128)(2,1)}), bf16[32768,256]{1,0:T(8,128)(2,1)}) %all-gather.4.cloned.1.call-update) | async-done | bytes 16777232 | tf_op jit(solution)/shard_map/all_gather | solution.py:15
  129.6 181.9 %while.13 = (s32[]{:T(128)}, bf16[64,128,256]{2,1,0:T(8,128)(2,1)}, s32[64]{0:T(128)S(1)}, bf16[32768,256]{1,0:T(8,128)(2,1)}, s32[]{:T(128)}, /*index=5*/s32[]{:T(128)}, s32[1]{0:T(128)}, s32[]{:T(128)}, s32[]{:T(128)}) while((s32[]{:T(128)}, bf16[64,128,256]{2,1,0:T(8,128)(2,1)}, s32[64]{0:T(128)S(1)}, bf16[32768,256]{1,0:T(8,128)(2,1)}, ...), condition=%wide.region_1.0_spmd, body=%wide.region_0.0_spmd.sunk | while | flops 8 | bytes 131763 | solution.py:24
  131.0 1.5 bitcast_dynamic-update-slice_fusion.2
  133.8 1.5 bitcast_dynamic-update-slice_fusion.2
  136.7 1.5 bitcast_dynamic-update-slice_fusion.2
  139.5 1.5 bitcast_dynamic-update-slice_fusion.2
  142.4 1.5 bitcast_dynamic-update-slice_fusion.2
  153.7 1.5 bitcast_dynamic-update-slice_fusion.2
  156.6 1.5 bitcast_dynamic-update-slice_fusion.2
  159.4 1.5 bitcast_dynamic-update-slice_fusion.2
  162.3 1.5 bitcast_dynamic-update-slice_fusion.2
  165.1 1.5 bitcast_dynamic-update-slice_fusion.2
  168.0 1.5 bitcast_dynamic-update-slice_fusion.2
  170.8 1.5 bitcast_dynamic-update-slice_fusion.2
  173.6 1.5 bitcast_dynamic-update-slice_fusion.2
  176.5 1.5 bitcast_dynamic-update-slice_fusion.2
  179.3 1.5 bitcast_dynamic-update-slice_fusion.2
  182.2 1.5 bitcast_dynamic-update-slice_fusion.2
  185.0 1.5 bitcast_dynamic-update-slice_fusion.2
  187.9 1.5 bitcast_dynamic-update-slice_fusion.2
  190.7 1.5 bitcast_dynamic-update-slice_fusion.2
  193.5 1.5 bitcast_dynamic-update-slice_fusion.2
  196.4 1.5 bitcast_dynamic-update-slice_fusion.2
  199.2 1.5 bitcast_dynamic-update-slice_fusion.2
  202.1 1.5 bitcast_dynamic-update-slice_fusion.2
  204.9 1.5 bitcast_dynamic-update-slice_fusion.2
  207.8 1.5 bitcast_dynamic-update-slice_fusion.2
  210.6 1.5 bitcast_dynamic-update-slice_fusion.2
  213.4 1.5 bitcast_dynamic-update-slice_fusion.2
  216.3 1.5 bitcast_dynamic-update-slice_fusion.2
  222.0 1.5 bitcast_dynamic-update-slice_fusion.2
  224.8 1.5 bitcast_dynamic-update-slice_fusion.2
  227.6 1.5 bitcast_dynamic-update-slice_fusion.2
  230.5 1.5 bitcast_dynamic-update-slice_fusion.2
  233.3 1.5 bitcast_dynamic-update-slice_fusion.2
  236.2 1.5 bitcast_dynamic-update-slice_fusion.2
  239.0 1.5 bitcast_dynamic-update-slice_fusion.2
  241.9 1.5 bitcast_dynamic-update-slice_fusion.2
  244.7 1.5 bitcast_dynamic-update-slice_fusion.2
  247.5 1.5 bitcast_dynamic-update-slice_fusion.2
  250.4 1.5 bitcast_dynamic-update-slice_fusion.2
  253.2 1.5 bitcast_dynamic-update-slice_fusion.2
  256.1 1.5 bitcast_dynamic-update-slice_fusion.2
  261.8 1.5 bitcast_dynamic-update-slice_fusion.2
  264.6 1.5 bitcast_dynamic-update-slice_fusion.2
  267.5 1.5 bitcast_dynamic-update-slice_fusion.2
  270.3 1.5 bitcast_dynamic-update-slice_fusion.2
  273.1 1.5 bitcast_dynamic-update-slice_fusion.2
  276.0 1.5 bitcast_dynamic-update-slice_fusion.2
  278.8 1.5 bitcast_dynamic-update-slice_fusion.2
  281.7 1.5 bitcast_dynamic-update-slice_fusion.2
  284.5 1.5 bitcast_dynamic-update-slice_fusion.2
  287.3 1.5 bitcast_dynamic-update-slice_fusion.2
  290.2 1.5 bitcast_dynamic-update-slice_fusion.2
  293.0 1.5 bitcast_dynamic-update-slice_fusion.2
  298.7 1.5 bitcast_dynamic-update-slice_fusion.2
  301.5 1.5 bitcast_dynamic-update-slice_fusion.2
  304.4 1.5 bitcast_dynamic-update-slice_fusion.2
  307.2 1.5 bitcast_dynamic-update-slice_fusion.2
  310.1 1.5 bitcast_dynamic-update-slice_fusion.2
  311.5 8.2 %gather_fusion = bf16[96,128,256]{2,1,0:T(8,128)(2,1)} fusion(bf16[64,128,256]{2,1,0:T(8,128)(2,1)} %get-tuple-element.84, s32[1024]{0:T(1024)S(1)} %pad_clamp_fusion), kind=kCustom, calls=%fused_computation | custom fusion | bytes 12583296 | tf_op jit(solution)/shard_map/gather | solution.py:29
  319.7 4.8 %fusion.1 = (f32[256]{0:T(256)S(1)}, f32[4,256,128]{1,2,0:T(8,128)S(1)}) fusion(bf16[4,24,128,128]{3,2,1,0:T(8,128)(2,1)} %all-gather.6.cloned.1.call-done, bf16[4,24,128,256]{3,2,1,0:T(8,128)(2,1)} %bitcast.24), kind=kOutput, calls=%fused_computation.8 | convolution fusion | flops 805568256 | bytes 9962496 | tf_op jit(solution)/shard_map/isab,isbw->iaw/dot_general | solution.py:30
  324.6 123.7 %psum.7 = f32[256]{0:T(256)S(1)} all-reduce(f32[256]{0:T(256)S(1)} %get-tuple-element.93), channel_id=1, replica_groups=mesh['row'=64,'col'=12] {'row'}, use_global_device_ids=true, to_apply=%region_3.0 | all-reduce | flops 256 | bytes 2048 | tf_op jit(solution)/shard_map/psum | solution.py:34
  (84 shorter events, 53.9 us)
Async XLA Ops:
  6.5 29.5 %copy-start = (s32[64,64]{1,0:T(8,128)S(1)}, s32[64,64]{1,0:T(8,128)}, u32[]{:S(2)}) copy-start(s32[64,64]{1,0:T(8,128)} %param.8) | copy-start | bytes 49156
  6.5 123.1 %all-gather.4.cloned.1.call-start = ((), (), s32[]{:S(2)}) async-start(), calls=%async_computation | async-start | bytes 17039360 | tf_op jit(solution)/shard_map/all_gather | solution.py:15
  7.3 312.5 %all-gather.6.cloned.1.call-start = ((), (), s32[]{:S(2)}) async-start(), calls=%async_computation.1 | async-start | bytes 3407872 | tf_op jit(solution)/shard_map/all_gather | solution.py:27
Sparse Core Ops, SparseCore 0:
  11.3 118.2 all-gather.3
  132.0 55.0 all-gather.5
where the time goes:
time: 460 us; the launch traced here: 456 us
  blocking collectives  152 us (33%)
  local copies, waits for them, and re-layouts  145 us (32%)
  waiting for transfers between devices  94.8 us (21%)
  loops' own time  45.1 us (10%)
  between operations  13.4 us (3%)
  matrix products  4.84 us (1%)
    psum x1, blocking collectives, local(): column_sum = lax.psum(jnp.sum(squared, axis=(0, 1)), 'row')  124 us
    dynamic_update_slice x64, local copies, waits for them, and re-layouts, place(): return lax.dynamic_update_slice(held, picked[None], (step, zero, zero))  94.3 us
    all_gather x1, waiting for transfers between devices, local(): portion = lax.all_gather(stripe, 'row', axis=0, tiled=True)  93.4 us
    another operation x1, loops' own time, local(): lax.fori_loop(0, count, place, jnp.zeros((owners, tile_edge, stripe_width...  45.1 us
    dynamic_slice x64, local copies, waits for them, and re-layouts, place(): start = step * shard_rows + my_column[step] * tile_edge  42.5 us
    all_gather x1, blocking collectives, local(): owner_index = lax.all_gather(block_owner, 'col', axis=1, tiled=True)  27.9 us
  transfers between devices with their start and end apart: 2, of which 1 were waited for; matrix products, arithmetic and copies ran while one was open for 32% of the time, Pallas kernels for 0%

commit v1 on v0

v1 whole, which is shorter than its diff:
```python
import functools

import jax
import jax.numpy as jnp
from jax import lax
from jax.experimental import pallas as pl
from jax.experimental.pallas import tpu as pltpu
from jax.sharding import PartitionSpec as P

MESH = pl.DeviceIdType.MESH
NX, NY, NC = 4, 8, 2
FIRST = 32


def hops_of(n):
    return [(+1, 0, n // 2), (-1, 1, n // 2), (+1, 1, n // 2 - 1), (-1, 0, n // 2 - 1)]


def place_of(direction, hop, n):
    return hop if direction > 0 or hop == n // 2 else n // 2 + hop


def distance_of(place, n):
    return place if place <= n // 2 else -(place - n // 2)


def kernel(nz, a_ref, owner_ref, rows_ref, stripe_ref, out_ref, rows, ids_out, ids, ids_s, held, sent1, got1, sent2,
           got2, sums1, sums2, ysem, yrecv, zsem, zrecv, isem, irecv, xsem, xrecv, s1, r1, s2, r2, c1, d1, c2, d2,
           local_sem, *blocks):
    yb, xb = blocks[:NY], blocks[NY:]
    me, z = lax.axis_index("row"), lax.axis_index("col")
    y, x, c = me // (NX * NC), (me // NC) % NX, me % NC

    def row(dy, dx, dc):
        return ((y + dy + NY) % NY) * (NX * NC) + ((x + dx + NX) % NX) * NC + (c + dc) % NC

    def at(dy=0, dx=0, dc=0, dz=0):
        return (row(dy, dx, dc), (z + dz + nz) % nz)

    tiles, edge, width = stripe_ref.shape
    rest = edge - FIRST
    xg = [(dx, dc) for dx in range(NX) for dc in range(NC) if dx or dc]
    yg = [(dy, dc) for dy in range(NY) for dc in range(NC) if dy or dc]

    own = [
        pltpu.make_async_copy(rows_ref, rows, local_sem.at[0]),
        pltpu.make_async_copy(stripe_ref.at[:, pl.ds(FIRST, rest)], yb[0], local_sem.at[1]),
        pltpu.make_async_copy(stripe_ref.at[:, pl.ds(0, FIRST)], xb[0], local_sem.at[2]),
        pltpu.make_async_copy(a_ref, held.at[0], local_sem.at[3]),
    ]
    for copy in own:
        copy.start()
    ids_out[...] = jnp.zeros_like(ids_out)
    ids_out[0 : owner_ref.shape[0], 0 : owner_ref.shape[1]] = owner_ref[...]
    ids[0] = ids_out[...]

    barrier = pltpu.get_barrier_semaphore()
    met = [(0, dx, dc, 0) for dx, dc in xg] + [(dy, 0, dc, 0) for dy, dc in yg] + [(0, 0, 0, 1), (0, 0, 0, -1)]
    for dy, dx, dc, dz in met:
        pl.semaphore_signal(barrier, inc=1, device_id=at(-dy, -dx, dc, -dz), device_id_type=MESH)
    pl.semaphore_wait(barrier, len(met))

    started = []

    def send(src, dst, send_sem, recv_sem, device):
        copy = pltpu.make_async_remote_copy(
            src_ref=src, dst_ref=dst, send_sem=send_sem, recv_sem=recv_sem, device_id=device, device_id_type=MESH
        )
        copy.start()
        started.append(copy)
        return copy

    half = tiles // 2
    arriving = {}

    def y_send(lane, hop):
        direction, chunk, _ = hops_of(NY)[lane]
        part = pl.ds(chunk * half, half)
        if hop == 0:
            src = stripe_ref.at[part, pl.ds(FIRST, rest)]
        else:
            src = yb[place_of(direction, hop, NY)].at[part]
        arriving["y", lane, hop + 1] = send(
            src, yb[place_of(direction, hop + 1, NY)].at[part], ysem.at[lane, hop], yrecv.at[lane, hop],
            at(dy=direction))

    def z_send(lane, hop):
        direction, chunk, _ = hops_of(nz)[lane]
        part = pl.ds(chunk * half, half)
        src = a_ref.at[part] if hop == 0 else held.at[place_of(direction, hop, nz), part]
        arriving["z", lane, hop + 1] = send(
            src, held.at[place_of(direction, hop + 1, nz), part], zsem.at[lane, hop], zrecv.at[lane, hop],
            at(dz=direction))

    def i_send(lane, hop):
        direction = hops_of(nz)[lane][0]
        src = ids_out if hop == 0 else ids.at[place_of(direction, hop, nz)]
        arriving["i", lane, hop + 1] = send(
            src, ids.at[place_of(direction, hop + 1, nz)], isem.at[lane, hop], irecv.at[lane, hop], at(dz=direction))

    def last(kind, lane):
        if kind == "i":
            return nz // 2 if lane == 0 else nz // 2 - 1
        return hops_of(NY if kind == "y" else nz)[lane][2]

    senders = {"y": y_send, "z": z_send, "i": i_send}

    def arrive(kind, lane, hop):
        if hop <= last(kind, lane):
            arriving[kind, lane, hop].wait_recv()
            if hop < last(kind, lane):
                senders[kind](lane, hop)

    def give1(place):
        block = yb[place]
        dy = -distance_of(place, NY)
        owner = row(dy, 0, 0)
        for n, (dx, dc) in enumerate(xg):
            slot = place * len(xg) + n
            sent1[slot] = block[rows[owner, row(0, dx, dc)]]
            pltpu.make_async_remote_copy(
                src_ref=sent1.at[slot], dst_ref=got1.at[owner], send_sem=s1, recv_sem=r1, device_id=at(0, dx, dc),
                device_id_type=MESH).start()
        got1[owner] = block[rows[owner, me]]

    def from_x(dx, dc=0):
        return y * (NX * NC) + ((x + dx + NX) % NX) * NC + (c + dc) % NC

    def slot2(yy, xx, cc):
        return (yy * NC + cc) * NX + xx

    def give2():
        for n, (dy, dc) in enumerate(yg):
            there = row(dy, 0, dc)
            for dx in range(NX):
                xx = (x + dx) % NX
                sent2[n * NX + xx] = xb[dx][rows[from_x(dx), there]]
            pltpu.make_async_remote_copy(
                src_ref=sent2.at[pl.ds(n * NX, NX)], dst_ref=got2.at[pl.ds(slot2(y, 0, c), NX)], send_sem=s2,
                recv_sem=r2, device_id=at(dy, 0, dc), device_id_type=MESH).start()
        for dx in range(NX):
            got2[slot2(y, (x + dx) % NX, c)] = xb[dx][rows[from_x(dx), me]]

    for lane in range(4):
        y_send(lane, 0)
        z_send(lane, 0)
    x_sent = [
        send(stripe_ref.at[:, pl.ds(0, FIRST)], xb[dx], xsem.at[dx - 1], xrecv.at[dx - 1], at(dx=-dx))
        for dx in range(1, NX)
    ]
    i_send(0, 0)
    i_send(1, 0)
    for copy in own:
        copy.wait()
    give1(0)
    for hop in range(1, nz // 2 + 1):
        for pair in (0, 2):
            for kind in ("y", "z") if hop <= NY // 2 else ("z",):
                for lane in (pair, pair + 1):
                    arrive(kind, lane, hop)
        arrive("i", 0, hop)
        arrive("i", 1, hop)
        if hop < NY // 2:
            give1(place_of(1, hop, NY))
            give1(place_of(-1, hop, NY))
        elif hop == NY // 2:
            give1(hop)
        if hop == 1:
            for copy in x_sent:
                copy.wait_recv()
            give2()

    copy = pltpu.make_async_copy(ids, ids_s, local_sem.at[4])
    copy.start()
    copy.wait()
    n1, n2 = NY * len(xg), len(yg) * NX
    pltpu.make_async_copy(got1.at[pl.ds(0, n1)], got1.at[pl.ds(0, n1)], r1).wait()
    pltpu.make_async_copy(got2.at[pl.ds(0, n2)], got2.at[pl.ds(0, n2)], r2).wait()

    def multiply(p, total):
        acc = jnp.zeros((edge, width), jnp.float32)
        for h in range(nz):
            parts = []
            for s in range(2):
                o = ids_s[h, p, s]
                parts += [got2[slot2(o // (NX * NC), (o // NC) % NX, o % NC)], got1[o]]
            left = jnp.concatenate([held[h, p, 0], held[h, p, 1]], axis=1)
            acc += jnp.dot(left, jnp.concatenate(parts, axis=0), preferred_element_type=jnp.float32)
        squared = acc * acc
        out_ref[p] = squared
        return total + jnp.sum(squared.reshape(edge // 8, 8, width), axis=0)

    total = lax.fori_loop(0, tiles, multiply, jnp.zeros((8, width), jnp.float32))

    sums1[0] = total
    copies = [
        send(sums1.at[0], sums1.at[n + 1], c1.at[n], d1.at[n], at(0, dx, dc)) for n, (dx, dc) in enumerate(xg)
    ]
    for copy in copies:
        copy.wait_recv()
    sums2[0] = jnp.sum(sums1[...], axis=0)
    copies = [send(sums2.at[0], sums2.at[dy], c2.at[dy - 1], d2.at[dy - 1], at(dy)) for dy in range(1, NY)]
    for copy in copies:
        copy.wait_recv()
    column_sum = jnp.sum(jnp.sum(sums2[...], axis=0), axis=0, keepdims=True)

    row_count = float(NY * NX * NC * tiles * edge)

    def scale(p, _):
        out_ref[p] = row_count * out_ref[p] / column_sum
        return 0

    lax.fori_loop(0, tiles, scale, 0)
    for copy in started:
        copy.wait_send()
    pltpu.make_async_copy(sent1, sent1, s1).wait()
    pltpu.make_async_copy(sent2, sent2, s2).wait()


def solution(mesh):
    nz = mesh.shape["col"]
    n_xg, n_yg = NX * NC - 1, NY * NC - 1

    def local(a_tiles, block_owner, send_rows, stripe):
        tiles, slots, edge, _ = a_tiles.shape
        width = stripe.shape[1]
        rest = edge - FIRST
        vmem, any_ = pl.BlockSpec(memory_space=pltpu.VMEM), pl.BlockSpec(memory_space=pl.ANY)
        dma, bf16 = pltpu.SemaphoreType.DMA, jnp.bfloat16
        out = pl.pallas_call(
            functools.partial(kernel, nz),
            out_shape=jax.ShapeDtypeStruct((tiles, edge, width), jnp.float32),
            in_specs=[any_, vmem, any_, any_],
            out_specs=vmem,
            scratch_shapes=[
                pltpu.SMEM(send_rows.shape, jnp.int32),
                pltpu.VMEM((8, 128), jnp.int32),
                pltpu.VMEM((nz, 8, 128), jnp.int32),
                pltpu.SMEM((nz, 8, 128), jnp.int32),
                pltpu.VMEM((nz, tiles, slots, edge, edge), bf16),
                pltpu.VMEM((NY * n_xg, rest, width), bf16),
                pltpu.VMEM((NY * NX * NC, rest, width), bf16),
                pltpu.VMEM((n_yg * NX, FIRST, width), bf16),
                pltpu.VMEM((NY * NX * NC, FIRST, width), bf16),
                pltpu.VMEM((n_xg + 1, 8, width), jnp.float32),
                pltpu.VMEM((NY, 8, width), jnp.float32),
                dma((4, NY // 2)), dma((4, NY // 2)),
                dma((4, nz // 2)), dma((4, nz // 2)),
                dma((2, nz // 2)), dma((2, nz // 2)),
                dma((NX - 1,)), dma((NX - 1,)),
                dma, dma, dma, dma,
                dma((n_xg,)), dma((n_xg,)),
                dma((NY - 1,)), dma((NY - 1,)),
                dma((5,)),
            ]
            + [pltpu.VMEM((tiles, rest, width), bf16)] * NY
            + [pltpu.VMEM((tiles, FIRST, width), bf16)] * NX,
            compiler_params=pltpu.CompilerParams(
                collective_id=0, has_side_effects=True, vmem_limit_bytes=40 * 2**20
            ),
            name="expand",
        )(a_tiles, block_owner, send_rows, stripe.reshape(tiles, edge, width))
        return out.reshape(tiles * edge, width)

    placed = (P("row", "col", None, None), P("row", "col"), P(), P("row", "col"))
    return jax.shard_map(local, mesh=mesh, in_specs=placed, out_specs=P("row", "col"), check_vma=False)
```

time: 460 us -> 90.2 us (0.20)
  blocking collectives: 152 us -> 0 us
  local copies, waits for them, and re-layouts: 145 us -> 4.22 us
  waiting for transfers between devices: 94.8 us -> 0 us
  Pallas kernels: 0 us -> 85.6 us
  loops' own time: 45.1 us -> 0 us
  between operations: 13.4 us -> 0.01 us
  matrix products: 4.84 us -> 0 us
    psum x1 -> x0, blocking collectives: 124 us -> none  [local(): column_sum = lax.psum(jnp.sum(squared, axis=(0, 1)), 'row')]
    dynamic_update_slice x64 -> x0, local copies, waits for them, and re-layouts: 94.3 us -> none  [place(): return lax.dynamic_update_slice(held, picked[None], (step, zero, zero))]
    all_gather x2 -> x0, waiting for transfers between devices: 93.4 us -> none  [the longest x1 93.4 us: local(): portion = lax.all_gather(stripe, 'row', axis=0, tiled=True)]
    pallas_call x0 -> x1, Pallas kernels: none -> 85.6 us  [local(): pl.pallas_call(functools.partial(kernel, nz), out_shape=jax.ShapeDtypeStr...]
    another operation x1 -> x0, loops' own time: 45.1 us -> none  [local(): lax.fori_loop(0, count, place, jnp.zeros((owners, tile_edge, stripe_width...]
    dynamic_slice x65 -> x0, local copies, waits for them, and re-layouts: 42.7 us -> none  [the longest x64 42.5 us: place(): start = step * shard_rows + my_column[step] * tile_edge]
    all_gather x1 -> x0, blocking collectives: 27.9 us -> none  [local(): owner_index = lax.all_gather(block_owner, 'col', axis=1, tiled=True)]
    gather x1 -> x0, local copies, waits for them, and re-layouts: 8.19 us -> none  [local(): right_tiles = fetched[owner_index]]
  transfers between devices with their start and end apart: 2 -> 0, of which waited for: 1 -> 0; matrix products, arithmetic and copies ran while one was open for 32% -> 0% of each run, Pallas kernels for 0% -> 0%
where the time goes in v1:
time: 90.2 us; the launch traced here: 89.9 us
  Pallas kernels  85.6 us (95%)
  local copies, waits for them, and re-layouts  4.22 us (5%)
    pallas_call x1, Pallas kernels, local(): pl.pallas_call(functools.partial(kernel, nz), out_shape=jax.ShapeDtypeStr...  85.6 us
    unnamed x10, local copies, waits for them, and re-layouts  4.22 us

profile of v1, /device:TPU:1, one launch (start us, length us, event | category | flops | bytes accessed | tf_op | source)
XLA Modules:
  0.0 89.9 jit_solution(3613435612668679079)
XLA Ops:
  0.0 0.0 copy-start.3
  0.0 0.7 copy-done.3
  0.7 0.1 copy.5.owner_ref
  0.8 0.0 copy-start
  0.8 0.9 %copy-done = bf16[4,2,128,128]{3,2,1,0:T(8,128)(2,1)S(1)} copy-done((bf16[4,2,128,128]{3,2,1,0:T(8,128)(2,1)S(1)}, bf16[4,2,128,128]{3,2,1,0:T(8,128)(2,1)}, u32[]{:S(2)}) %copy-start) | copy-done | bytes 262168
  1.7 0.0 copy-start.1
  1.7 0.9 %copy-done.1 = bf16[512,256]{1,0:T(8,128)(2,1)S(1)} copy-done((bf16[512,256]{1,0:T(8,128)(2,1)S(1)}, bf16[512,256]{1,0:T(8,128)(2,1)}, u32[]{:S(2)}) %copy-start.1) | copy-done | bytes 262168
  2.7 0.0 copy-start.2
  2.7 0.8 copy-done.2
  3.4 85.6 %expand.1 = f32[4,128,256]{2,1,0:T(8,128)S(1)} custom-call(bf16[4,2,128,128]{3,2,1,0:T(8,128)(2,1)S(1)} %copy-done, s32[4,2]{1,0:T(4,128)S(1)} %copy.5.owner_ref, s32[64,64]{1,0:T(8,128)S(1)} %copy-done.2, bf16[4,128,256]{2,1,0:T(8,128)(2,1)S(1)} %bitcast.3), custom_call_target="tpu_custom_call" | custom-call | tf_op jit(solution)/shard_map/expand/pallas_call | solution.py:230
  89.1 0.8 copy.7
Async XLA Ops:
  0.0 0.7 copy-start.3
  0.8 0.9 %copy-start = (bf16[4,2,128,128]{3,2,1,0:T(8,128)(2,1)S(1)}, bf16[4,2,128,128]{3,2,1,0:T(8,128)(2,1)}, u32[]{:S(2)}) copy-start(bf16[4,2,128,128]{3,2,1,0:T(8,128)(2,1)} %a_ref.1) | copy-start | bytes 786436
  1.7 0.9 %copy-start.1 = (bf16[512,256]{1,0:T(8,128)(2,1)S(1)}, bf16[512,256]{1,0:T(8,128)(2,1)}, u32[]{:S(2)}) copy-start(bf16[512,256]{1,0:T(8,128)(2,1)} %param.7) | copy-start | bytes 786436
  2.7 0.8 copy-start.2

commit v2 on v1

v2 whole, which is shorter than its diff:
```python
import functools

import jax
import jax.numpy as jnp
from jax import lax
from jax.experimental import pallas as pl
from jax.experimental.pallas import tpu as pltpu
from jax.sharding import PartitionSpec as P

MESH = pl.DeviceIdType.MESH
VMEM = 60 * 2**20
NX, NY, NC = 4, 8, 2
EARLY = 4
FIRST = 32


def hops_of(n):
    return [(+1, 0, n // 2), (-1, 1, n // 2), (+1, 1, n // 2 - 1), (-1, 0, n // 2 - 1)]


def place_of(direction, hop, n):
    return hop if direction > 0 or hop == n // 2 else n // 2 + hop


def distance_of(place, n):
    return place if place <= n // 2 else -(place - n // 2)


def kernel(nz, a_ref, owner_ref, rows_ref, stripe_ref, out_ref, rows, owners, ids_out, ids, ids_s, held, sent1, got1,
           sent2, got2, sums1, sums2, ysem, yrecv, zsem, zrecv, isem, irecv, xsem, xrecv, s1, r1, s2, r2, c1, d1, c2, d2,
           local_sem, plane_in, ring_in, *blocks):
    yb, xb = blocks[:NY], blocks[NY:]
    me, z = lax.axis_index("row"), lax.axis_index("col")
    y, x, c = me // (NX * NC), (me // NC) % NX, me % NC

    def row(dy, dx, dc):
        return ((y + dy + NY) % NY) * (NX * NC) + ((x + dx + NX) % NX) * NC + (c + dc) % NC

    def at(dy=0, dx=0, dc=0, dz=0):
        return (row(dy, dx, dc), (z + dz + nz) % nz)

    tiles, edge, width = stripe_ref.shape
    rest = edge - FIRST
    xg = [(dx, dc) for dx in (2, 1, 3, 0) for dc in range(NC) if dx or dc]
    yg = [(dy, dc) for dy in (4, 3, 5, 2, 6, 1, 7, 0) for dc in range(NC) if dy or dc]

    own = [
        pltpu.make_async_copy(rows_ref, rows, local_sem.at[0]),
        pltpu.make_async_copy(stripe_ref.at[:, pl.ds(FIRST, rest)], yb[0], local_sem.at[1]),
        pltpu.make_async_copy(stripe_ref.at[:, pl.ds(0, FIRST)], xb[0], local_sem.at[2]),
        pltpu.make_async_copy(a_ref, held.at[0], local_sem.at[3]),
        pltpu.make_async_copy(owner_ref, owners, local_sem.at[4]),
    ]
    for copy in own:
        copy.start()

    barrier = pltpu.get_barrier_semaphore()

    def tell(dz, dy, dx, core):
        there = ((y + dy + NY) % NY) * (NX * NC) + ((x + dx + NX) % NX) * NC + core
        pl.semaphore_signal(barrier, inc=1, device_id=(there, (z + dz + nz) % nz), device_id_type=MESH)

    plane = [(dy, 0) for dy in range(1, NY)] + [(0, dx) for dx in range(1, NX)]
    for dy, dx in plane:
        tell(0, dy, dx, 0)
    tell(1, 0, 0, 1)
    tell(-1, 0, 0, 1)

    @pl.when(c == 1)
    def _():
        tell(0, 0, 0, 0)

    ids_out[...] = jnp.zeros_like(ids_out)
    own.pop().wait()
    ids_out[0 : owners.shape[0], 0 : owners.shape[1]] = owners[...]
    ids[0] = ids_out[...]

    @pl.when(c == 0)
    def _():
        pl.semaphore_wait(barrier, 2 * len(plane) + 1)
        pl.semaphore_signal(plane_in, inc=1, device_id=at(dc=1), device_id_type=MESH)

    @pl.when(c == 1)
    def _():
        pl.semaphore_wait(plane_in, 1)

    def meet_ring():
        @pl.when(c == 1)
        def _():
            pl.semaphore_wait(barrier, 4)
            pl.semaphore_signal(ring_in, inc=1, device_id=at(dc=1), device_id_type=MESH)

        @pl.when(c == 0)
        def _():
            pl.semaphore_wait(ring_in, 1)

    def remote(src, dst, send_sem, recv_sem, device):
        return pltpu.make_async_remote_copy(
            src_ref=src, dst_ref=dst, send_sem=send_sem, recv_sem=recv_sem, device_id=device, device_id_type=MESH
        )

    half = tiles // 2

    def y_copy(lane, hop):
        direction, chunk, _ = hops_of(NY)[lane]
        part = pl.ds(chunk * half, half)
        if hop == 0:
            src = stripe_ref.at[part, pl.ds(FIRST, rest)]
        else:
            src = yb[place_of(direction, hop, NY)].at[part]
        dst = yb[place_of(direction, hop + 1, NY)].at[part]
        return remote(src, dst, ysem, yrecv.at[lane, hop], at(dy=direction))

    def z_copy(lane, hop):
        direction, chunk, _ = hops_of(nz)[lane]
        part = pl.ds(chunk * half, half)
        src = a_ref.at[part] if hop == 0 else held.at[place_of(direction, hop, nz), part]
        dst = held.at[place_of(direction, hop + 1, nz), part]
        return remote(src, dst, zsem, zrecv.at[lane, hop], at(dz=direction))

    def i_copy(lane, hop):
        direction = hops_of(nz)[lane][0]
        src = ids_out if hop == 0 else ids.at[place_of(direction, hop, nz)]
        dst = ids.at[place_of(direction, hop + 1, nz)]
        return remote(src, dst, isem, irecv.at[lane, hop], at(dz=direction))

    def arrive(copy_of, lane, hop, last):
        if hop <= last:
            copy_of(lane, hop - 1).wait_recv()
            if hop < last:
                copy_of(lane, hop).start()

    def give1(place):
        block = yb[place]
        owner = row(-distance_of(place, NY), 0, 0)
        for n, (dx, dc) in enumerate(xg):
            slot = place * len(xg) + n
            sent1[slot] = block[rows[owner, row(0, dx, dc)]]
            remote(sent1.at[slot], got1.at[owner], s1, r1, at(0, dx, dc)).start()
        got1[owner] = block[rows[owner, me]]

    def from_x(dx):
        return row(0, dx, 0)

    def slot2(yy, xx, cc):
        return (yy * NC + cc) * NX + xx

    def give2(first, stop):
        for n, (dy, dc) in list(enumerate(yg))[max(first, 0) : max(stop, 0)]:
            there = row(dy, 0, dc)
            for dx in range(NX):
                sent2[n * NX + (x + dx) % NX] = xb[dx][rows[from_x(dx), there]]
            remote(sent2.at[pl.ds(n * NX, NX)], got2.at[pl.ds(slot2(y, 0, c), NX)], s2, r2, at(dy, 0, dc)).start()

    def x_copy(dx):
        return remote(stripe_ref.at[:, pl.ds(0, FIRST)], xb[dx], xsem, xrecv.at[dx - 1], at(dx=-dx))

    def start_ring():
        meet_ring()
        for lane in range(4):
            z_copy(lane, 0).start()
        i_copy(0, 0).start()
        i_copy(1, 0).start()

    def y_step(hop):
        for lane in range(4):
            arrive(y_copy, lane, hop, hops_of(NY)[lane][2])

    def z_step(hop):
        for lane in range(4):
            arrive(z_copy, lane, hop, hops_of(nz)[lane][2])
        for lane in range(2):
            arrive(i_copy, lane, hop, nz // 2 - lane)

    def x_step():
        for dx in range(1, NX):
            x_copy(dx).wait_recv()
        for dx in range(NX):
            got2[slot2(y, (x + dx) % NX, c)] = xb[dx][rows[from_x(dx), me]]

    for lane in range(4):
        y_copy(lane, 0).start()
    for dx in range(1, NX):
        x_copy(dx).start()

    def run(start, offset):
        if start == 0:
            start_ring()
        for copy in own:
            copy.wait()
        give1(0)
        done = 0
        for hop in range(1, NY // 2 + 1):
            y_step(hop)
            if start == hop:
                start_ring()
            if hop > offset:
                done += 1
                z_step(done)
            if hop == 2:
                x_step()
            give2(5 * hop - 10, 5 * hop - 5)
            give1(place_of(1, hop, NY))
            if hop < NY // 2:
                give1(place_of(-1, hop, NY))
        for hop in range(done + 1, nz // 2 + 1):
            z_step(hop)

    @pl.when(z == 0)
    def _():
        run(1, 1)

    @pl.when((z > 0) & (z < EARLY))
    def _():
        run(1, 1)

    @pl.when(z >= EARLY)
    def _():
        run(0, 0)

    copy = pltpu.make_async_copy(ids, ids_s, local_sem.at[4])
    copy.start()
    copy.wait()
    n1, n2 = NY * len(xg), len(yg) * NX
    pltpu.make_async_copy(got2.at[pl.ds(0, n2)], got2.at[pl.ds(0, n2)], r2).wait()
    pltpu.make_async_copy(got1.at[pl.ds(0, n1)], got1.at[pl.ds(0, n1)], r1).wait()

    def multiply(p, total):
        acc = jnp.zeros((edge, width), jnp.float32)
        for h in range(nz):
            parts = []
            for s in range(2):
                o = ids_s[h, s, p]
                parts += [got2[slot2(o // (NX * NC), (o // NC) % NX, o % NC)], got1[o]]
            left = jnp.concatenate([held[h, p, 0], held[h, p, 1]], axis=1)
            acc += jnp.dot(left, jnp.concatenate(parts, axis=0), preferred_element_type=jnp.float32)
        squared = acc * acc
        out_ref[p] = squared
        return total + jnp.sum(squared.reshape(edge // 8, 8, width), axis=0)

    total = lax.fori_loop(0, tiles, multiply, jnp.zeros((8, width), jnp.float32))

    sums1[0] = total
    for n, (dx, dc) in enumerate(xg):
        remote(sums1.at[0], sums1.at[n + 1], c1, d1, at(0, dx, dc)).start()
    pltpu.make_async_copy(sums1.at[pl.ds(1, len(xg))], sums1.at[pl.ds(1, len(xg))], d1).wait()
    sums2[0] = jnp.sum(sums1[...], axis=0)
    for dy in (4, 3, 5, 2, 6, 1, 7):
        remote(sums2.at[0], sums2.at[dy], c2, d2, at(dy)).start()
    pltpu.make_async_copy(sums2.at[pl.ds(1, NY - 1)], sums2.at[pl.ds(1, NY - 1)], d2).wait()
    column_sum = jnp.sum(jnp.sum(sums2[...], axis=0), axis=0, keepdims=True)
    row_count = float(NY * NX * NC * tiles * edge)

    def scale(p, _):
        out_ref[p] = row_count * out_ref[p] / column_sum
        return 0

    lax.fori_loop(0, tiles, scale, 0)

    for ref, sem in (
        (sent1, s1), (sent2, s2), (sums1.at[pl.ds(1, len(xg))], c1), (sums2.at[pl.ds(1, NY - 1)], c2),
        (sent1.at[pl.ds(0, (NY - 1) * tiles)], ysem), (sent2.at[pl.ds(0, (NX - 1) * tiles)], xsem),
        (held.at[pl.ds(1, nz - 1)], zsem), (ids.at[pl.ds(1, nz - 1)], isem),
    ):
        pltpu.make_async_copy(ref, ref, sem).wait()


def solution(mesh):
    nz = mesh.shape["col"]
    n_xg, n_yg = NX * NC - 1, NY * NC - 1

    def local(a_tiles, block_owner, send_rows, stripe):
        tiles, slots, edge, _ = a_tiles.shape
        width = stripe.shape[1]
        rest = edge - FIRST
        vmem, hbm = pl.BlockSpec(memory_space=pltpu.VMEM), pl.BlockSpec(memory_space=pltpu.MemorySpace.HBM)
        dma, bf16 = pltpu.SemaphoreType.DMA, jnp.bfloat16
        out = pl.pallas_call(
            functools.partial(kernel, nz),
            out_shape=jax.ShapeDtypeStruct((tiles, edge, width), jnp.float32),
            in_specs=[hbm, hbm, hbm, hbm],
            out_specs=vmem,
            scratch_shapes=[
                pltpu.SMEM(send_rows.shape, jnp.int32),
                pltpu.VMEM((slots, tiles), jnp.int32),
                pltpu.VMEM((8, 128), jnp.int32),
                pltpu.VMEM((nz, 8, 128), jnp.int32),
                pltpu.SMEM((nz, 8, 128), jnp.int32),
                pltpu.VMEM((nz, tiles, slots, edge, edge), bf16),
                pltpu.VMEM((NY * n_xg, rest, width), bf16),
                pltpu.VMEM((NY * NX * NC, rest, width), bf16),
                pltpu.VMEM((n_yg * NX, FIRST, width), bf16),
                pltpu.VMEM((NY * NX * NC, FIRST, width), bf16),
                pltpu.VMEM((n_xg + 1, 8, width), jnp.float32),
                pltpu.VMEM((NY, 8, width), jnp.float32),
                dma, dma((4, NY // 2)),
                dma, dma((4, nz // 2)),
                dma, dma((2, nz // 2)),
                dma, dma((NX - 1,)),
                dma, dma, dma, dma, dma, dma, dma, dma,
                dma((5,)),
                pltpu.SemaphoreType.REGULAR,
                pltpu.SemaphoreType.REGULAR,
            ]
            + [pltpu.VMEM((tiles, rest, width), bf16)] * NY
            + [pltpu.VMEM((tiles, FIRST, width), bf16)] * NX,
            compiler_params=pltpu.CompilerParams(
                collective_id=0, has_side_effects=True, vmem_limit_bytes=VMEM
            ),
            name="expand",
        )(a_tiles, block_owner.T, send_rows, stripe.reshape(tiles, edge, width))
        return out.reshape(tiles * edge, width)

    placed = (P("row", "col", None, None), P("row", "col"), P(), P("row", "col"))
    return jax.shard_map(local, mesh=mesh, in_specs=placed, out_specs=P("row", "col"), check_vma=False)
```

time: 90.2 us -> 78 us (0.86)
  Pallas kernels: 85.6 us -> 75.9 us
  local copies, waits for them, and re-layouts: 4.22 us -> 1.87 us
    pallas_call x1, Pallas kernels: 85.6 us -> 75.9 us  [local(): pl.pallas_call(functools.partial(kernel, nz), out_shape=jax.ShapeDtypeStr...]
    unnamed x10 -> x1, local copies, waits for them, and re-layouts: 4.22 us -> 1.87 us
where the time goes in v2:
time: 78 us; the launch traced here: 77.8 us
  Pallas kernels  75.9 us (97%)
  local copies, waits for them, and re-layouts  1.87 us (2%)
    pallas_call x1, Pallas kernels, local(): pl.pallas_call(functools.partial(kernel, nz), out_shape=jax.ShapeDtypeStr...  75.9 us
    unnamed x1, local copies, waits for them, and re-layouts  1.87 us

profile of v2, /device:TPU:1, one launch (start us, length us, event | category | flops | bytes accessed | tf_op | source)
XLA Modules:
  0.0 77.8 jit_solution(5812173429346002428)
XLA Ops:
  0.0 75.9 %expand.1 = f32[4,128,256]{2,1,0:T(8,128)} custom-call(bf16[4,2,128,128]{3,2,1,0:T(8,128)(2,1)} %a_ref.1, s32[2,4]{1,0:T(2,128)} %bitcast.5, s32[64,64]{1,0:T(8,128)} %rows_ref.1, bf16[4,128,256]{2,1,0:T(8,128)(2,1)} %bitcast.4), custom_call_target="tpu_custom_call" | custom-call | tf_op jit(solution)/shard_map/expand/pallas_call | solution.py:278
  75.9 1.9 %copy.6 = f32[512,256]{1,0:T(8,128)} copy(f32[512,256]{1,0:T(8,128)} %bitcast.3) | data formatting | bytes 1048576

commit v3 on v2

v3 whole, which is shorter than its diff:
```python
import functools

import jax
import jax.numpy as jnp
from jax import lax
from jax.experimental import pallas as pl
from jax.experimental.pallas import tpu as pltpu
from jax.sharding import PartitionSpec as P

MESH = pl.DeviceIdType.MESH
FIRST_PLANE = (
    "o u Y1 y1", "g1 s Y2 w", "r y2 g2 Z1", "x t0 z1 t1", "Y3 y3 Z2 g3", "z2 t2 Z3 Y4",
    "g4 z3 t3 Z4", "z4 Z5 z5",
)
EARLY_PLANES = (
    "o u s Y1", "y1 w r g1", "Y2 Z1 y2 z1", "g2 x t0 Z2", "Y3 t1 y3 z2", "g3 t2 Z3 Y4",
    "z3 g4 Z4 t3", "z4 Z5 z5",
)
LATE_PLANES = (
    "s o u w", "r Y1 Z1 y1", "z1 g1 Y2 Z2", "y2 z2 g2 x", "t0 Z3 Y3 t1", "y3 z3 g3 t2",
    "Z4 Y4 z4 g4", "Z5 t3 z5",
)
VMEM = 62 * 2**20
NX, NY, NC = 4, 8, 2
EARLY = 4
FIRST = 32


def hops_of(n):
    return [(+1, 0, n // 2), (-1, 1, n // 2), (+1, 1, n // 2 - 1), (-1, 0, n // 2 - 1)]


def ring_of(n):
    return [(+1, 0, n // 2 - 1), (-1, 1, n // 2), (+1, 1, n // 2 - 1), (-1, 0, n // 2)]


def place_of(direction, hop, n):
    return hop if direction > 0 or hop == n // 2 else n // 2 + hop


def distance_of(place, n):
    return place if place <= n // 2 else -(place - n // 2)


def kernel(nz, a_ref, owner_ref, rows_ref, stripe_ref, out_ref, rows, owners, ids_out, ids, ids_s, held, sent1, got1,
           sent2, got2, sums1, sums2, ysem, yrecv, zsem, zfirst, zrecv, isem, irecv, xsem, xrecv, s1, r1, s2, r2, c1, d1, c2, d2,
           local_sem, plane_in, ring_in, *blocks):
    yb, xb = blocks[:NY], blocks[NY:]
    me, z = lax.axis_index("row"), lax.axis_index("col")
    y, x, c = lax.div(me, NX * NC), lax.rem(lax.div(me, NC), NX), lax.rem(me, NC)

    def row(dy, dx, dc):
        return lax.rem(y + (dy + NY), NY) * (NX * NC) + lax.rem(x + (dx + NX), NX) * NC + lax.rem(c + dc, NC)

    def at(dy=0, dx=0, dc=0, dz=0):
        return (row(dy, dx, dc), lax.rem(z + (dz + nz), nz) if dz else z)

    tiles, edge, width = stripe_ref.shape
    rest = edge - FIRST
    xg = [(dx, dc) for dx in (2, 1, 3, 0) for dc in range(NC) if dx or dc]
    yg = [(dy, dc) for dy in (0, 1, 7, 2, 6, 3, 5, 4) for dc in range(NC) if dy or dc]

    own = [
        pltpu.make_async_copy(rows_ref, rows, local_sem.at[0]),
        pltpu.make_async_copy(stripe_ref.at[:, pl.ds(FIRST, rest)], yb[0], local_sem.at[1]),
        pltpu.make_async_copy(stripe_ref.at[:, pl.ds(0, FIRST)], xb[0], local_sem.at[2]),
        pltpu.make_async_copy(a_ref, held.at[0], local_sem.at[3]),
        pltpu.make_async_copy(owner_ref, owners, local_sem.at[4]),
    ]
    for copy in own:
        copy.start()

    barrier = pltpu.get_barrier_semaphore()

    def tell(dz, dy, dx, core):
        there, level = at(dy, dx, 0, dz)
        pl.semaphore_signal(barrier, inc=1, device_id=(there - c + core, level), device_id_type=MESH)

    plane = [(1, 0), (-1, 0)] + [(0, dx) for dx in range(1, NX)]
    for dy, dx in plane:
        tell(0, dy, dx, 0)
    tell(1, 0, 0, 1)
    tell(-1, 0, 0, 1)

    @pl.when(c == 1)
    def _():
        tell(0, 0, 0, 0)

    ids_out[...] = jnp.zeros_like(ids_out)
    own.pop().wait()
    ids_out[0 : owners.shape[0], 0 : owners.shape[1]] = owners[...]
    ids[0] = ids_out[...]

    @pl.when(c == 0)
    def _():
        pl.semaphore_wait(barrier, 2 * len(plane) + 1)
        pl.semaphore_signal(plane_in, inc=1, device_id=at(dc=1), device_id_type=MESH)

    @pl.when(c == 1)
    def _():
        pl.semaphore_wait(plane_in, 1)

    def meet_ring():
        @pl.when(c == 1)
        def _():
            pl.semaphore_wait(barrier, 4)
            pl.semaphore_signal(ring_in, inc=1, device_id=at(dc=1), device_id_type=MESH)

        @pl.when(c == 0)
        def _():
            pl.semaphore_wait(ring_in, 1)

    def remote(src, dst, send_sem, recv_sem, device):
        return pltpu.make_async_remote_copy(
            src_ref=src, dst_ref=dst, send_sem=send_sem, recv_sem=recv_sem, device_id=device, device_id_type=MESH
        )

    half = tiles // 2

    def y_copy(lane, hop):
        direction, chunk, _ = hops_of(NY)[lane]
        part = pl.ds(chunk * half, half)
        if hop == 0:
            src = stripe_ref.at[part, pl.ds(FIRST, rest)]
        else:
            src = yb[place_of(direction, hop, NY)].at[part]
        dst = yb[place_of(direction, hop + 1, NY)].at[part]
        return remote(src, dst, ysem, yrecv.at[lane, hop], at(dy=direction))

    def z_copy(lane, hop):
        direction, chunk, _ = ring_of(nz)[lane]
        part = pl.ds(chunk * half, half)
        src = a_ref.at[part] if hop == 0 else held.at[place_of(direction, hop, nz), part]
        dst = held.at[place_of(direction, hop + 1, nz), part]
        return remote(src, dst, zfirst if hop == 0 and lane < 2 else zsem, zrecv.at[lane, hop], at(dz=direction))

    def i_copy(lane, hop):
        direction = ring_of(nz)[lane][0]
        src = ids_out if hop == 0 else ids.at[place_of(direction, hop, nz)]
        dst = ids.at[place_of(direction, hop + 1, nz)]
        return remote(src, dst, isem, irecv.at[lane, hop], at(dz=direction))

    def arrive(copy_of, lane, hop, last):
        if hop <= last:
            copy_of(lane, hop - 1).wait_recv()
            if hop < last:
                copy_of(lane, hop).start()

    def slot1(k):
        return jnp.where(k > NY // 2, 2 * (NY - k), jnp.maximum(2 * k - 1, 0))

    def give1(hop):
        places = [place_of(1, hop, NY)] + ([place_of(-1, hop, NY)] if 0 < hop < NY // 2 else [])
        first = max(2 * hop - 1, 0)
        owners_y = [row(-distance_of(place, NY), 0, 0) for place in places]
        mine = (x * NC + c) * NY + first
        for n, (dx, dc) in enumerate(xg):
            there = row(0, dx, dc)
            for k, (place, owner) in enumerate(zip(places, owners_y)):
                sent1[n * NY + first + k] = yb[place][rows[owner, there]]
            remote(sent1.at[pl.ds(n * NY + first, len(places))], got1.at[pl.ds(mine, len(places))], s1, r1,
                   at(0, dx, dc)).start()
        for k, (place, owner) in enumerate(zip(places, owners_y)):
            got1[mine + k] = yb[place][rows[owner, me]]

    def from_x(dx):
        return row(0, dx, 0)

    def slot2(yy, xx, cc):
        return (yy * NC + cc) * NX + xx

    def give2(first, stop):
        for n, (dy, dc) in list(enumerate(yg))[first:stop]:
            there = row(dy, 0, dc)
            for dx in range(NX):
                sent2[n * NX + lax.rem(x + dx, NX)] = xb[dx][rows[from_x(dx), there]]
            remote(sent2.at[pl.ds(n * NX, NX)], got2.at[pl.ds(slot2(y, 0, c), NX)], s2, r2, at(dy, 0, dc)).start()

    def x_copy(dx):
        return remote(stripe_ref.at[:, pl.ds(0, FIRST)], xb[dx], xsem, xrecv.at[dx - 1], at(dx=-dx))

    def start_ring():
        meet_ring()
        for lane in range(2):
            i_copy(lane, 0).start()
            z_copy(lane, 0).start()

    def y_step(hop, second):
        for lane in (2, 3) if second else (0, 1):
            arrive(y_copy, lane, hop, hops_of(NY)[lane][2])

    def z_step(hop, second):
        for lane in (2, 3) if second else (0, 1):
            last = ring_of(nz)[lane][2]
            if hop <= last:
                z_copy(lane, hop - 1).wait_recv()
            if not second:
                arrive(i_copy, lane, hop, nz // 2 - 1 + lane)
            if hop < last:
                z_copy(lane, hop).start()

    def x_step():
        for dx in range(1, NX):
            x_copy(dx).wait_recv()
        for dx in range(NX):
            got2[slot2(y, lax.rem(x + dx, NX), c)] = xb[dx][rows[from_x(dx), me]]

    for lane in range(2):
        y_copy(lane, 0).start()
    for dx in range(1, NX):
        x_copy(dx).start()

    def run(order):
        for step in [step for part in order for step in part.split()]:
            kind, n = step[0], int(step[1:] or 0)
            if kind == "s":
                start_ring()
            elif kind == "w":
                pltpu.make_async_copy(held.at[0], held.at[0], zfirst).wait()
            elif kind == "r":
                z_copy(2, 0).start()
                z_copy(3, 0).start()
            elif kind == "u":
                y_copy(2, 0).start()
                y_copy(3, 0).start()
            elif kind == "o":
                for copy in own:
                    copy.wait()
                give1(0)
            elif kind in "Yy":
                y_step(n, kind == "y")
            elif kind in "Zz":
                z_step(n, kind == "z")
            elif kind == "x":
                x_step()
            elif kind == "t":
                give2(*((0, 5), (5, 9), (9, 13), (13, 15))[n])
            elif kind == "g":
                give1(n)

    @pl.when(z == 0)
    def _():
        run(FIRST_PLANE)

    @pl.when((z > 0) & (z < EARLY))
    def _():
        run(EARLY_PLANES)

    @pl.when(z >= EARLY)
    def _():
        run(LATE_PLANES)

    n1, n2 = NY * len(xg), len(yg) * NX
    far = nz // 2
    near = [pltpu.make_async_copy(ids.at[h], ids_s.at[h], local_sem.at[h]) for h in range(nz) if h != far]
    for copy in near:
        copy.start()
    for copy in near:
        copy.wait()
    pltpu.make_async_copy(got2.at[pl.ds(0, n2)], got2.at[pl.ds(0, n2)], r2).wait()
    pltpu.make_async_copy(got1.at[pl.ds(0, n1)], got1.at[pl.ds(0, n1)], r1).wait()

    def partial(p, blocks_of_a):
        acc = jnp.zeros((edge, width), jnp.float32)
        for h in blocks_of_a:
            parts = []
            for s in range(2):
                o = ids_s[h, s, p]
                oy, ox, oc = o >> 3, (o >> 1) & 3, o & 1
                parts += [got2[slot2(oy, ox, oc)], got1[(ox * NC + oc) * NY + slot1((y - oy) & (NY - 1))]]
            left = jnp.concatenate([held[h, p, 0], held[h, p, 1]], axis=1)
            acc += jnp.dot(left, jnp.concatenate(parts, axis=0), preferred_element_type=jnp.float32)
        return acc

    def most(p, _):
        out_ref[p] = partial(p, [h for h in range(nz) if h != far])
        return 0

    lax.fori_loop(0, tiles, most, 0)
    i_copy(1, far - 1).wait_recv()
    copy = pltpu.make_async_copy(ids.at[far], ids_s.at[far], local_sem.at[far])
    copy.start()
    for lane in (1, 3):
        z_copy(lane, far - 1).wait_recv()
    copy.wait()

    def finish(p, total):
        acc = out_ref[p] + partial(p, [far])
        squared = acc * acc
        out_ref[p] = squared
        return total + jnp.sum(squared.reshape(edge // 8, 8, width), axis=0)

    total = lax.fori_loop(0, tiles, finish, jnp.zeros((8, width), jnp.float32))

    sums1[0] = jnp.sum(total, axis=0, keepdims=True)
    for n, (dx, dc) in enumerate(xg):
        remote(sums1.at[0], sums1.at[n + 1], c1, d1, at(0, dx, dc)).start()
    pltpu.make_async_copy(sums1.at[pl.ds(1, len(xg))], sums1.at[pl.ds(1, len(xg))], d1).wait()
    sums2[0] = jnp.sum(sums1[...], axis=0)
    for dy in (4, 3, 5, 2, 6, 1, 7):
        remote(sums2.at[0], sums2.at[dy], c2, d2, at(dy)).start()
    pltpu.make_async_copy(sums2.at[pl.ds(1, NY - 1)], sums2.at[pl.ds(1, NY - 1)], d2).wait()
    column_sum = jnp.sum(sums2[...], axis=0)
    row_count = float(NY * NX * NC * tiles * edge)

    def scale(p, _):
        out_ref[p] = row_count * out_ref[p] / column_sum
        return 0

    lax.fori_loop(0, tiles, scale, 0)

    for ref, sem in (
        (sent1, s1), (sent2, s2), (sums1.at[pl.ds(1, len(xg))], c1), (sums2.at[pl.ds(1, NY - 1)], c2),
        (sent1.at[pl.ds(0, (NY - 1) * tiles)], ysem), (sent2.at[pl.ds(0, (NX - 1) * tiles)], xsem),
        (held.at[pl.ds(1, nz - 2)], zsem), (ids.at[pl.ds(1, nz - 1)], isem),
    ):
        pltpu.make_async_copy(ref, ref, sem).wait()


def solution(mesh):
    nz = mesh.shape["col"]
    n_xg, n_yg = NX * NC - 1, NY * NC - 1

    def local(a_tiles, block_owner, send_rows, stripe):
        tiles, slots, edge, _ = a_tiles.shape
        width = stripe.shape[1]
        rest = edge - FIRST
        vmem, hbm = pl.BlockSpec(memory_space=pltpu.VMEM), pl.BlockSpec(memory_space=pltpu.MemorySpace.HBM)
        dma, bf16 = pltpu.SemaphoreType.DMA, jnp.bfloat16
        out = pl.pallas_call(
            functools.partial(kernel, nz),
            out_shape=pltpu.VMEM((tiles, edge, width), jnp.float32),
            in_specs=[hbm, hbm, hbm, hbm],
            out_specs=vmem,
            scratch_shapes=[
                pltpu.SMEM(send_rows.shape, jnp.int32),
                pltpu.VMEM((slots, tiles), jnp.int32),
                pltpu.VMEM((8, 128), jnp.int32),
                pltpu.VMEM((nz, 8, 128), jnp.int32),
                pltpu.SMEM((nz, 8, 128), jnp.int32),
                pltpu.VMEM((nz, tiles, slots, edge, edge), bf16),
                pltpu.VMEM((NY * n_xg, rest, width), bf16),
                pltpu.VMEM((NY * NX * NC, rest, width), bf16),
                pltpu.VMEM((n_yg * NX, FIRST, width), bf16),
                pltpu.VMEM((NY * NX * NC, FIRST, width), bf16),
                pltpu.VMEM((n_xg + 1, 1, width), jnp.float32),
                pltpu.VMEM((NY, 1, width), jnp.float32),
                dma, dma((4, NY // 2)),
                dma, dma, dma((4, nz // 2)),
                dma, dma((2, nz // 2)),
                dma, dma((NX - 1,)),
                dma, dma, dma, dma, dma, dma, dma, dma,
                dma((nz,)),
                pltpu.SemaphoreType.REGULAR,
                pltpu.SemaphoreType.REGULAR,
            ]
            + [pltpu.VMEM((tiles, rest, width), bf16)] * NY
            + [pltpu.VMEM((tiles, FIRST, width), bf16)] * NX,
            compiler_params=pltpu.CompilerParams(
                collective_id=0, has_side_effects=True, vmem_limit_bytes=VMEM
            ),
            name="expand",
        )(a_tiles, block_owner.T, send_rows, stripe.reshape(tiles, edge, width))
        return out.reshape(tiles * edge, width)

    placed = (P("row", "col", None, None), P("row", "col"), P(), P("row", "col"))
    return jax.shard_map(local, mesh=mesh, in_specs=placed, out_specs=P("row", "col"), check_vma=False)
```

time: 78 us -> 65.6 us (0.84)
  Pallas kernels: 75.9 us -> 64.6 us
  local copies, waits for them, and re-layouts: 1.87 us -> 0.8 us
    pallas_call x1, Pallas kernels: 75.9 us -> 64.6 us  [local(): pl.pallas_call(functools.partial(kernel, nz), out_shape=pltpu.VMEM((tiles...]
    unnamed x1, local copies, waits for them, and re-layouts: 1.87 us -> 0.8 us
where the time goes in v3:
time: 65.6 us; the launch traced here: 65.4 us
  Pallas kernels  64.6 us (98%)
  local copies, waits for them, and re-layouts  0.8 us (1%)
    pallas_call x1, Pallas kernels, local(): pl.pallas_call(functools.partial(kernel, nz), out_shape=pltpu.VMEM((tiles...  64.6 us

profile of v3, /device:TPU:1, one launch (start us, length us, event | category | flops | bytes accessed | tf_op | source)
XLA Modules:
  0.0 65.4 jit_solution(1038026451013774365)
XLA Ops:
  0.0 64.6 %expand.1 = f32[4,128,256]{2,1,0:T(8,128)S(1)} custom-call(bf16[4,2,128,128]{3,2,1,0:T(8,128)(2,1)} %a_ref.1, s32[2,4]{1,0:T(2,128)} %bitcast.5, s32[64,64]{1,0:T(8,128)} %rows_ref.1, bf16[4,128,256]{2,1,0:T(8,128)(2,1)} %bitcast.4), custom_call_target="tpu_custom_call" | custom-call | tf_op jit(solution)/shard_map/expand/pallas_call | solution.py:330
  64.6 0.8 %copy.6 = f32[512,256]{1,0:T(8,128)} copy(f32[512,256]{1,0:T(8,128)S(1)} %bitcast.3) | data formatting | bytes 1048576

commit v4 on v3

--- a/solution.py
+++ b/solution.py
@@ -9,15 +9,15 @@
 
 MESH = pl.DeviceIdType.MESH
 FIRST_PLANE = (
-    "o u Y1 y1", "g1 s Y2 w", "r y2 g2 Z1", "x t0 z1 t1", "Y3 y3 Z2 g3", "z2 t2 Z3 Y4",
+    "o u Y1 y1", "g1 s r Y2", "y2 w g2 Z1", "x t0 z1 t1", "Y3 y3 Z2 g3", "z2 t2 Z3 Y4",
     "g4 z3 t3 Z4", "z4 Z5 z5",
 )
 EARLY_PLANES = (
-    "o u s Y1", "y1 w r g1", "Y2 Z1 y2 z1", "g2 x t0 Z2", "Y3 t1 y3 z2", "g3 t2 Z3 Y4",
+    "o u s r", "Y1 y1 g1 w", "Y2 Z1 y2 z1", "g2 x t0 Z2", "Y3 t1 y3 z2", "g3 t2 Z3 Y4",
     "z3 g4 Z4 t3", "z4 Z5 z5",
 )
 LATE_PLANES = (
-    "s o u w", "r Y1 Z1 y1", "z1 g1 Y2 Z2", "y2 z2 g2 x", "t0 Z3 Y3 t1", "y3 z3 g3 t2",
+    "s o u r", "Y1 Z1 y1 z1", "g1 w Y2 Z2", "y2 z2 g2 x", "t0 Z3 Y3 t1", "y3 z3 g3 t2",
     "Z4 Y4 z4 g4", "Z5 t3 z5",
 )
 VMEM = 62 * 2**20
@@ -293,14 +293,14 @@
     total = lax.fori_loop(0, tiles, finish, jnp.zeros((8, width), jnp.float32))
 
     sums1[0] = jnp.sum(total, axis=0, keepdims=True)
-    for n, (dx, dc) in enumerate(xg):
-        remote(sums1.at[0], sums1.at[n + 1], c1, d1, at(0, dx, dc)).start()
-    pltpu.make_async_copy(sums1.at[pl.ds(1, len(xg))], sums1.at[pl.ds(1, len(xg))], d1).wait()
-    sums2[0] = jnp.sum(sums1[...], axis=0)
-    for dy in (4, 3, 5, 2, 6, 1, 7):
-        remote(sums2.at[0], sums2.at[dy], c2, d2, at(dy)).start()
-    pltpu.make_async_copy(sums2.at[pl.ds(1, NY - 1)], sums2.at[pl.ds(1, NY - 1)], d2).wait()
-    column_sum = jnp.sum(sums2[...], axis=0)
+    far_first = sorted(
+        ((dy, dx, dc) for dy in range(NY) for dx in range(NX) for dc in range(NC) if dy or dx or dc),
+        key=lambda o: -min(o[0], NY - o[0]) - min(o[1], NX - o[1]),
+    )
+    for n, (dy, dx, dc) in enumerate(far_first):
+        remote(sums1.at[0], sums1.at[n + 1], c1, d1, at(dy, dx, dc)).start()
+    pltpu.make_async_copy(sums1.at[pl.ds(1, len(far_first))], sums1.at[pl.ds(1, len(far_first))], d1).wait()
+    column_sum = jnp.sum(sums1[...], axis=0)
     row_count = float(NY * NX * NC * tiles * edge)
 
     def scale(p, _):
@@ -310,7 +310,7 @@
     lax.fori_loop(0, tiles, scale, 0)
 
     for ref, sem in (
-        (sent1, s1), (sent2, s2), (sums1.at[pl.ds(1, len(xg))], c1), (sums2.at[pl.ds(1, NY - 1)], c2),
+        (sent1, s1), (sent2, s2), (sums1.at[pl.ds(1, len(far_first))], c1),
         (sent1.at[pl.ds(0, (NY - 1) * tiles)], ysem), (sent2.at[pl.ds(0, (NX - 1) * tiles)], xsem),
         (held.at[pl.ds(1, nz - 2)], zsem), (ids.at[pl.ds(1, nz - 1)], isem),
     ):
@@ -343,7 +343,7 @@
                 pltpu.VMEM((NY * NX * NC, rest, width), bf16),
                 pltpu.VMEM((n_yg * NX, FIRST, width), bf16),
                 pltpu.VMEM((NY * NX * NC, FIRST, width), bf16),
-                pltpu.VMEM((n_xg + 1, 1, width), jnp.float32),
+                pltpu.VMEM((NY * NX * NC, 1, width), jnp.float32),
                 pltpu.VMEM((NY, 1, width), jnp.float32),
                 dma, dma((4, NY // 2)),
                 dma, dma, dma((4, nz // 2)),

time: 65.6 us -> 64.6 us (0.985)
  Pallas kernels: 64.6 us -> 63.6 us
    pallas_call x1, Pallas kernels: 64.6 us -> 63.6 us  [local(): pl.pallas_call(functools.partial(kernel, nz), out_shape=pltpu.VMEM((tiles...]
where the time goes in v4:
time: 64.6 us; the launch traced here: 64.5 us
  Pallas kernels  63.6 us (98%)
  local copies, waits for them, and re-layouts  0.8 us (1%)
    pallas_call x1, Pallas kernels, local(): pl.pallas_call(functools.partial(kernel, nz), out_shape=pltpu.VMEM((tiles...  63.6 us

profile of v4, /device:TPU:1, one launch (start us, length us, event | category | flops | bytes accessed | tf_op | source)
XLA Modules:
  0.0 64.5 jit_solution(18076691326654219032)
XLA Ops:
  0.0 63.6 %expand.1 = f32[4,128,256]{2,1,0:T(8,128)S(1)} custom-call(bf16[4,2,128,128]{3,2,1,0:T(8,128)(2,1)} %a_ref.1, s32[2,4]{1,0:T(2,128)} %bitcast.5, s32[64,64]{1,0:T(8,128)} %rows_ref.1, bf16[4,128,256]{2,1,0:T(8,128)(2,1)} %bitcast.4), custom_call_target="tpu_custom_call" | custom-call | tf_op jit(solution)/shard_map/expand/pallas_call | solution.py:330
  63.7 0.8 %copy.6 = f32[512,256]{1,0:T(8,128)} copy(f32[512,256]{1,0:T(8,128)S(1)} %bitcast.3) | data formatting | bytes 1048576

commit v5 on v4

--- a/solution.py
+++ b/solution.py
@@ -189,6 +189,9 @@
         for lane in (2, 3) if second else (0, 1):
             arrive(y_copy, lane, hop, hops_of(NY)[lane][2])
 
+    def near_copy(h):
+        return pltpu.make_async_copy(ids.at[h], ids_s.at[h], local_sem.at[h])
+
     def z_step(hop, second):
         for lane in (2, 3) if second else (0, 1):
             last = ring_of(nz)[lane][2]
@@ -196,6 +199,9 @@
                 z_copy(lane, hop - 1).wait_recv()
             if not second:
                 arrive(i_copy, lane, hop, nz // 2 - 1 + lane)
+                place = place_of(ring_of(nz)[lane][0], hop, nz)
+                if place != nz // 2:
+                    near_copy(place).start()
             if hop < last:
                 z_copy(lane, hop).start()
 
@@ -226,6 +232,7 @@
             elif kind == "o":
                 for copy in own:
                     copy.wait()
+                near_copy(0).start()
                 give1(0)
             elif kind in "Yy":
                 y_step(n, kind == "y")
@@ -252,11 +259,9 @@
 
     n1, n2 = NY * len(xg), len(yg) * NX
     far = nz // 2
-    near = [pltpu.make_async_copy(ids.at[h], ids_s.at[h], local_sem.at[h]) for h in range(nz) if h != far]
-    for copy in near:
-        copy.start()
-    for copy in near:
-        copy.wait()
+    for h in range(nz):
+        if h != far:
+            near_copy(h).wait()
     pltpu.make_async_copy(got2.at[pl.ds(0, n2)], got2.at[pl.ds(0, n2)], r2).wait()
     pltpu.make_async_copy(got1.at[pl.ds(0, n1)], got1.at[pl.ds(0, n1)], r1).wait()
 

time: 64.6 us -> 64.6 us (level)
  no operation moved by 1% of the time
where the time goes in v5:
time: 64.6 us; the launch traced here: 64.5 us
  Pallas kernels  63.7 us (99%)
  local copies, waits for them, and re-layouts  0.8 us (1%)
    pallas_call x1, Pallas kernels, local(): pl.pallas_call(functools.partial(kernel, nz), out_shape=pltpu.VMEM((tiles...  63.7 us

profile of v5, /device:TPU:1, one launch (start us, length us, event | category | flops | bytes accessed | tf_op | source)
XLA Modules:
  0.0 64.5 jit_solution(8701214930947856767)
XLA Ops:
  0.0 63.7 %expand.1 = f32[4,128,256]{2,1,0:T(8,128)S(1)} custom-call(bf16[4,2,128,128]{3,2,1,0:T(8,128)(2,1)} %a_ref.1, s32[2,4]{1,0:T(2,128)} %bitcast.5, s32[64,64]{1,0:T(8,128)} %rows_ref.1, bf16[4,128,256]{2,1,0:T(8,128)(2,1)} %bitcast.4), custom_call_target="tpu_custom_call" | custom-call | tf_op jit(solution)/shard_map/expand/pallas_call | solution.py:335
  63.7 0.8 %copy.6 = f32[512,256]{1,0:T(8,128)} copy(f32[512,256]{1,0:T(8,128)S(1)} %bitcast.3) | data formatting | bytes 1048576

commit v6 on v5

--- a/solution.py
+++ b/solution.py
@@ -9,8 +9,7 @@
 
 MESH = pl.DeviceIdType.MESH
 FIRST_PLANE = (
-    "o u Y1 y1", "g1 s r Y2", "y2 w g2 Z1", "x t0 z1 t1", "Y3 y3 Z2 g3", "z2 t2 Z3 Y4",
-    "g4 z3 t3 Z4", "z4 Z5 z5",
+    "o u Y1 y1", "g1 s r Y2", "y2 w g2 Z1", "x t0 z1 Y3", "t1 y3 Z2 g3", "z2 t2 Z3 Y4", "z3 g4 Z4 t3", "z4 Z5 z5",
 )
 EARLY_PLANES = (
     "o u s r", "Y1 y1 g1 w", "Y2 Z1 y2 z1", "g2 x t0 Z2", "Y3 t1 y3 z2", "g3 t2 Z3 Y4",

time: 64.6 us -> 64.6 us (level)
  no operation moved by 1% of the time
where the time goes in v6:
time: 64.6 us; the launch traced here: 64.5 us
  Pallas kernels  63.7 us (99%)
  local copies, waits for them, and re-layouts  0.8 us (1%)
    pallas_call x1, Pallas kernels, local(): pl.pallas_call(functools.partial(kernel, nz), out_shape=pltpu.VMEM((tiles...  63.7 us

profile of v6, /device:TPU:1, one launch (start us, length us, event | category | flops | bytes accessed | tf_op | source)
XLA Modules:
  0.0 64.5 jit_solution(16624339931127656048)
XLA Ops:
  0.0 63.7 %expand.1 = f32[4,128,256]{2,1,0:T(8,128)S(1)} custom-call(bf16[4,2,128,128]{3,2,1,0:T(8,128)(2,1)} %a_ref.1, s32[2,4]{1,0:T(2,128)} %bitcast.5, s32[64,64]{1,0:T(8,128)} %rows_ref.1, bf16[4,128,256]{2,1,0:T(8,128)(2,1)} %bitcast.4), custom_call_target="tpu_custom_call" | custom-call | tf_op jit(solution)/shard_map/expand/pallas_call | solution.py:334
  63.7 0.8 %copy.6 = f32[512,256]{1,0:T(8,128)} copy(f32[512,256]{1,0:T(8,128)S(1)} %bitcast.3) | data formatting | bytes 1048576
